TPU v7x, 256 devices: a whole 4x4x8 slice. The times are simulated.
256 devices in a mesh: frame: 32 (over y_hi, z, core), patch: 8 (over x, y_lo).
Axes of the slice: x: 4, y: 4 (y_hi: 2, y_lo: 2; y = y_hi * 2 + y_lo), z: 8, core: 2. Of those that a mesh axis runs over, the one named last changes fastest.
Arguments:
- tokens: bfloat16 [128, 1024, 1280], P('frame', 'patch'), may hold values from -6 to 6
- spatial_in: bfloat16 [1280, 1920], replicated, may hold values from -1 to 1
- spatial_out: bfloat16 [640, 1280], replicated, may hold values from -0.25 to 0.25
- temporal_in: bfloat16 [1280, 1920], P('frame'), may hold values from -1 to 1
- temporal_out: bfloat16 [640, 1280], P('frame'), may hold values from -0.25 to 0.25
- spatial_gain: float32 [1280], replicated, may hold values from 0.1 to 1.9
- temporal_gain: float32 [1280], replicated, may hold values from 0.1 to 1.9
- keep_masks: int32 [8, 2], replicated, may hold values from 0 to 1, as said below
Outputs:
- layer_out: bfloat16 [128, 1024, 1280], P('frame', 'patch')
Inputs may be any that keep to these rules, and one draw needn't show every extreme that they name: `keep_masks`: 1 keeps a video's branch, 0 drops it; in each branch at least one video keeps it and at least one drops it.
All inputs are finite; a program needn't handle non-finite values.
Results may differ from a plain program's by a relative error of at most 0.01.
Values may be sent and summed in bfloat16 or wider, within the bound.
A program may use at most 128 MiB of HBM per device.

v0:
```python
import jax
import jax.numpy as jnp
from jax import lax
from jax.sharding import PartitionSpec as P

HEADS = 8
HDIM = 80
CLIP_LEN = 16


keep_rate = 0.7


def normalize(values, gain):
    values = values.astype(jnp.float32)
    center = jnp.mean(values, axis=-1, keepdims=True)
    spread = jnp.mean(jnp.square(values - center), axis=-1, keepdims=True)
    return ((values - center) * lax.rsqrt(spread + 1e-06) * gain).astype(jnp.bfloat16)


def frame_coef(column, frame_count):
    frame_ids = lax.axis_index("frame") * frame_count + jnp.arange(frame_count)
    video_ids = frame_ids // CLIP_LEN
    match = (video_ids[:, None] == jnp.arange(column.shape[0])[None, :]).astype(jnp.float32)
    return jnp.sum(match * column.astype(jnp.float32)[None, :], axis=1) / keep_rate


def add_rows(portion, inputs):
    return jnp.dot(inputs, portion, preferred_element_type=jnp.float32)


def temporal_triple(normed_rows, temporal_in):
    empty = jnp.zeros((normed_rows.shape[0], temporal_in.shape[1]), jnp.float32)

    def accumulate(summed, portion, offset):
        return add_rows(portion, normed_rows)

    folded = accumulate(
        empty, lax.all_gather(temporal_in, "frame", axis=0, tiled=True), jnp.int32(0)
    )
    return folded.astype(jnp.bfloat16)


def temporal_project(mixed_rows, temporal_out):
    empty = jnp.zeros((mixed_rows.shape[0], temporal_out.shape[1]), jnp.float32)

    def accumulate(summed, portion, offset):
        return add_rows(portion, mixed_rows)

    return accumulate(
        empty, lax.all_gather(temporal_out, "frame", axis=0, tiled=True), jnp.int32(0)
    )


def temporal_mix(triple_pos):
    frames_all, columns = (triple_pos.shape[0], triple_pos.shape[1])
    videos = frames_all // CLIP_LEN
    parts = triple_pos.reshape(videos, CLIP_LEN, columns, 3, HEADS, HDIM)
    scores = jnp.einsum(
        "vfphd,vgphd->vphfg",
        parts[:, :, :, 0],
        parts[:, :, :, 1],
        preferred_element_type=jnp.float32,
    )
    chances = jax.nn.softmax(scores * HDIM ** (-0.5), axis=-1).astype(jnp.bfloat16)
    mixed = jnp.einsum(
        "vphfg,vgphd->vfphd", chances, parts[:, :, :, 2], preferred_element_type=jnp.float32
    )
    return mixed.astype(jnp.bfloat16).reshape(frames_all, columns, HEADS * HDIM)


def on_device(
    tokens,
    spatial_in,
    spatial_out,
    temporal_in,
    temporal_out,
    spatial_gain,
    temporal_gain,
    keep_masks,
):
    frames, patch_rows, width = tokens.shape
    inner = HEADS * HDIM
    normed = normalize(tokens, spatial_gain)
    triple = jnp.dot(
        normed.reshape(-1, width), spatial_in, preferred_element_type=jnp.float32
    ).astype(jnp.bfloat16)
    triple = triple.reshape(frames, patch_rows, 3 * inner)
    queries = triple[:, :, :inner].reshape(frames, patch_rows, HEADS, HDIM)
    gathered = lax.all_gather(triple[:, :, inner:], "patch", axis=1, tiled=True)
    all_patches = gathered.shape[1]
    keys = gathered[:, :, :inner].reshape(frames, all_patches, HEADS, HDIM)
    values_all = gathered[:, :, inner:].reshape(frames, all_patches, HEADS, HDIM)
    scores = jnp.einsum("fqhd,fkhd->fhqk", queries, keys, preferred_element_type=jnp.float32)
    chances = jax.nn.softmax(scores * HDIM ** (-0.5), axis=-1).astype(jnp.bfloat16)
    mixed = jnp.einsum("fhqk,fkhd->fqhd", chances, values_all, preferred_element_type=jnp.float32)
    mixed = mixed.astype(jnp.bfloat16).reshape(frames * patch_rows, inner)
    projected = jnp.dot(mixed, spatial_out, preferred_element_type=jnp.float32).reshape(
        frames, patch_rows, width
    )
    coef_space = frame_coef(keep_masks[:, 0], frames)
    after_space = (tokens.astype(jnp.float32) + coef_space[:, None, None] * projected).astype(
        jnp.bfloat16
    )
    moved = lax.all_to_all(after_space, "frame", split_axis=1, concat_axis=0, tiled=True)
    frames_all, columns = (moved.shape[0], moved.shape[1])
    normed_pos = normalize(moved, temporal_gain).reshape(-1, width)
    triple_pos = temporal_triple(normed_pos, temporal_in).reshape(frames_all, columns, 3 * inner)
    mixed_pos = temporal_mix(triple_pos)
    proj_pos = temporal_project(mixed_pos.reshape(-1, inner), temporal_out).reshape(
        frames_all, columns, width
    )
    coef_rows = jnp.repeat(
        keep_masks[:, 1].astype(jnp.float32) / keep_rate, CLIP_LEN, total_repeat_length=frames_all
    )
    result_pos = (moved.astype(jnp.float32) + coef_rows[:, None, None] * proj_pos).astype(
        jnp.bfloat16
    )
    result = lax.all_to_all(result_pos, "frame", split_axis=0, concat_axis=1, tiled=True)
    return result


def solution(mesh):
    placed = (
        P("frame", "patch", None),
        P(),
        P(),
        P("frame", None),
        P("frame", None),
        P(),
        P(),
        P(),
    )
    return jax.shard_map(
        on_device, mesh=mesh, in_specs=placed, out_specs=P("frame", "patch", None), check_vma=False
    )
```

profile of v0, /device:TPU:1, one launch (start us, length us, event | category | flops | bytes accessed | tf_op | source)
XLA Modules:
  0.0 493.9 jit_solution(6893528801119226764)
XLA Ops:
  10.6 5.3 %convolution_convert_fusion.1 = bf16[512,1920]{1,0:T(8,128)(2,1)S(1)} fusion(bf16[512,1280]{1,0:T(8,128)(2,1)S(1)} %bitcast.89, bf16[1280,1920]{1,0:T(8,128)(2,1)} %param.11), kind=kOutput, calls=%fused_computation.19 | convolution fusion | flops 2517565440 | bytes 8192000 | tf_op jit(solution)/shard_map/dot_general | solution.py:85
  24.2 208.3 %all-gather.5.cloned.1.call-done = bf16[4,1024,1280]{2,1,0:T(8,128)(2,1)} async-done(((bf16[4,128,1280]{2,1,0:T(8,128)(2,1)}), bf16[4,1024,1280]{2,1,0:T(8,128)(2,1)}) %all-gather.5.cloned.1.call-update) | async-done | bytes 10485776 | tf_op jit(solution)/shard_map/all_gather | solution.py:90
  232.5 9.0 %fusion.30 = (bf16[4,1024,640]{2,1,0:T(8,128)(2,1)}, bf16[4,1024,640]{2,1,0:T(8,128)(2,1)}) fusion(bf16[4,1024,1280]{2,1,0:T(8,128)(2,1)} %all-gather.5.cloned.1.call-done), kind=kLoop, calls=%fused_computation.62 | loop fusion | bytes 20971520 | tf_op jit(solution)/shard_map/slice | solution.py:92
  241.5 8.0 %copy.45 = bf16[4,1024,640]{1,2,0:T(8,128)(2,1)} copy(bf16[4,1024,640]{2,1,0:T(8,128)(2,1)} %get-tuple-element.18) | data formatting | bytes 10485760 | tf_op jit(solution)/shard_map/slice | solution.py:93
  249.5 8.0 %copy.47 = bf16[4,1024,640]{1,2,0:T(8,128)(2,1)} copy(bf16[4,1024,640]{2,1,0:T(8,128)(2,1)} %get-tuple-element.17) | data formatting | bytes 10485760 | tf_op jit(solution)/shard_map/slice | solution.py:92
  257.5 11.0 %fusion.33 = (f32[4,8,128]{2,1,0:T(8,128)S(1)}, f32[4,8,128,1024]{3,2,1,0:T(8,128)}) fusion(bf16[4,128,8,80]{1,3,2,0:T(8,128)(2,1)} %bitcast.86, bf16[4,1024,8,80]{1,3,2,0:T(8,128)(2,1)} %bitcast.82), kind=kOutput, calls=%fused_computation.65 | convolution fusion | flops 683672576 | bytes 22691840 | tf_op jit(solution)/shard_map/sub | solution.py:95
  268.5 10.4 %fusion.20 = bf16[4,8,80,128]{3,2,1,0:T(8,128)(2,1)S(1)} fusion(bf16[4,1024,8,80]{1,3,2,0:T(8,128)(2,1)} %bitcast.84, f32[4,8,128,1024]{3,2,1,0:T(8,128)} %get-tuple-element.31, f32[4,8,128]{2,1,0:T(8,128)S(1)} %get-tuple-element.30), kind=kOutput, calls=%fused_computation.34 | convolution fusion | flops 679804928 | bytes 22691840 | tf_op jit(solution)/shard_map/fhqk,fkhd->fqhd/dot_general | solution.py:96
  282.3 10.0 %all-to-all-start = ((bf16[4,128,1280]{2,0,1:T(4,128)(2,1)}), bf16[4,128,1280]{2,0,1:T(4,128)(2,1)S(1)}, u32[]{:S(2)}, u32[]{:S(2)}) async-start(bf16[4,128,1280]{2,0,1:T(4,128)(2,1)} %copy.49), calls=%async_computation | async-start | bytes 2621440 | tf_op jit(solution)/shard_map/all_to_all | solution.py:105
  293.1 5.0 %select_select_fusion = f32[128]{0:T(128)S(1)} fusion(pred[128]{0:T(512)(128)(4,1)S(1)} %copy-done.6, pred[128]{0:T(512)(128)(4,1)S(1)} %copy-done.7, pred[128]{0:T(512)(128)(4,1)S(1)} %copy-done.8, pred[128]{0:T(512)(128)(4,1)S(1)} %copy-done.9, pred[128]{0:T(512)(128)(4,1)S(1)} %copy-done.10, pred[128]{0:T(512)(128)(4,1)S(1)} %copy-done.11, ...), kind=kLoop, calls=%fused_computation.55 | loop fusion | flops 896 | bytes 1440 | tf_op jit(solution)/shard_map/jit(_take)/gather | solution.py:113
  298.1 25.6 %all-gather.9.cloned.1.call-done = bf16[32,20,1280]{2,1,0:T(8,128)(2,1)} async-done(((bf16[1,20,1280]{2,1,0:T(8,128)(2,1)}), bf16[32,20,1280]{2,1,0:T(8,128)(2,1)}) %all-gather.9.cloned.1.call-update) | async-done | bytes 1638416 | tf_op jit(solution)/shard_map/all_gather | solution.py:51
  323.7 3.6 reshape.200
  327.3 2.7 all-to-all-done
  332.5 4.0 reshape.159
  339.6 4.0 reshape.160
  343.6 2.4 fusion.29
  346.2 2.6 multiply_reduce_fusion.1
  348.9 64.3 %all-gather.7.cloned.1.call-done = bf16[1280,1920]{1,0:T(8,128)(2,1)} async-done(((bf16[40,1920]{1,0:T(8,128)(2,1)}), bf16[1280,1920]{1,0:T(8,128)(2,1)}) %all-gather.7.cloned.1.call-update) | async-done | bytes 4915216 | tf_op jit(solution)/shard_map/all_gather | solution.py:39
  413.2 7.5 %convolution_convert_fusion = bf16[512,1920]{1,0:T(8,128)(2,1)} fusion(bf16[1280,1920]{1,0:T(8,128)(2,1)} %all-gather.7.cloned.1.call-done, f32[512,1280]{1,0:T(8,128)} %reshape.160, f32[1280]{0:T(1024)S(1)} %copy-done.13, f32[512]{0:T(512)S(1)} %rsqrt.21, f32[512]{0:T(512)S(1)} %div.62), kind=kOutput, calls=%fused_computation.18 | convolution fusion | flops 2520186880 | bytes 9511936 | tf_op jit(solution)/shard_map/dot_general | solution.py:29
  420.7 6.4 %reshape_reshape.4 = bf16[8,16,4,3,8,80]{5,4,3,2,1,0:T(8,128)(2,1)} reshape(bf16[512,1920]{1,0:T(8,128)(2,1)} %convolution_convert_fusion) | data formatting | bytes 3932160 | tf_op jit(solution)/shard_map/reshape;reshape | solution.py:58
  427.1 3.9 fusion.31
  431.1 4.3 fusion.34
  438.9 2.7 dot_general.36
  441.6 3.1 fusion.10
  445.8 40.0 %all_to_all.27 = bf16[128,4,1280]{2,1,0:T(4,128)(2,1)S(1)} all-to-all(bf16[128,4,1280]{2,1,0:T(4,128)(2,1)S(1)} %copy.57), channel_id=1, replica_groups=mesh['frame'=32,'patch'=8] {'frame'}, dimensions={0} | all-to-all | bytes 2621440 | tf_op jit(solution)/shard_map/all_to_all | solution.py:119
  (65 shorter events, 28.4 us)
Async XLA Ops:
  6.5 272.4 %copy-start = (bf16[640,1280]{1,0:T(8,128)(2,1)S(1)}, bf16[640,1280]{1,0:T(8,128)(2,1)}, u32[]{:S(2)}) copy-start(bf16[640,1280]{1,0:T(8,128)(2,1)} %param.12) | copy-start | bytes 4915204
  6.5 3.5 copy-start.2
  6.5 3.6 copy-start.5
  6.5 225.9 %all-gather.5.cloned.1.call-start = ((), (), s32[]{:S(2)}) async-start(), calls=%async_computation.2 | async-start | bytes 11796480 | tf_op jit(solution)/shard_map/all_gather | solution.py:90
  15.9 1.3 copy-start.4
  18.3 5.7 %copy-start.14 = (s32[8,2]{0,1:T(2,128)S(1)}, s32[8,2]{0,1:T(2,128)}, u32[]{:S(2)}) copy-start(s32[8,2]{0,1:T(2,128)} %param.17) | copy-start | bytes 196
  18.3 305.4 %all-gather.9.cloned.1.call-start = ((), (), s32[]{:S(2)}) async-start(), calls=%async_computation.4 | async-start | bytes 2027520 | tf_op jit(solution)/shard_map/all_gather | solution.py:51
  19.0 394.2 %all-gather.7.cloned.1.call-start = ((), (), s32[]{:S(2)}) async-start(), calls=%async_computation.3 | async-start | bytes 5068800 | tf_op jit(solution)/shard_map/all_gather | solution.py:39
  280.2 12.9 %copy-start.6 = (pred[128]{0:T(512)(128)(4,1)S(1)}, pred[128]{0:T(512)(128)(4,1)}, u32[]{:S(2)}) copy-start(pred[128]{0:T(512)(128)(4,1)} %constant.138) | copy-start | bytes 388
  280.2 12.9 %copy-start.7 = (pred[128]{0:T(512)(128)(4,1)S(1)}, pred[128]{0:T(512)(128)(4,1)}, u32[]{:S(2)}) copy-start(pred[128]{0:T(512)(128)(4,1)} %constant.139) | copy-start | bytes 388
  280.2 12.8 %copy-start.8 = (pred[128]{0:T(512)(128)(4,1)S(1)}, pred[128]{0:T(512)(128)(4,1)}, u32[]{:S(2)}) copy-start(pred[128]{0:T(512)(128)(4,1)} %constant.140) | copy-start | bytes 388
  280.2 12.8 %copy-start.9 = (pred[128]{0:T(512)(128)(4,1)S(1)}, pred[128]{0:T(512)(128)(4,1)}, u32[]{:S(2)}) copy-start(pred[128]{0:T(512)(128)(4,1)} %constant.141) | copy-start | bytes 388
  280.2 12.8 %copy-start.10 = (pred[128]{0:T(512)(128)(4,1)S(1)}, pred[128]{0:T(512)(128)(4,1)}, u32[]{:S(2)}) copy-start(pred[128]{0:T(512)(128)(4,1)} %constant.142) | copy-start | bytes 388
  280.2 12.8 %copy-start.11 = (pred[128]{0:T(512)(128)(4,1)S(1)}, pred[128]{0:T(512)(128)(4,1)}, u32[]{:S(2)}) copy-start(pred[128]{0:T(512)(128)(4,1)} %constant.143) | copy-start | bytes 388
  280.3 12.8 %copy-start.12 = (pred[128]{0:T(512)(128)(4,1)S(1)}, pred[128]{0:T(512)(128)(4,1)}, u32[]{:S(2)}) copy-start(pred[128]{0:T(512)(128)(4,1)} %constant.144) | copy-start | bytes 388
  282.3 47.7 %all-to-all-start = ((bf16[4,128,1280]{2,0,1:T(4,128)(2,1)}), bf16[4,128,1280]{2,0,1:T(4,128)(2,1)S(1)}, u32[]{:S(2)}, u32[]{:S(2)}) async-start(bf16[4,128,1280]{2,0,1:T(4,128)(2,1)} %copy.49), calls=%async_computation | async-start | bytes 2621440 | tf_op jit(solution)/shard_map/all_to_all | solution.py:105
  337.3 2.4 copy-start.1
  343.6 69.6 %copy-start.13 = (f32[1280]{0:T(1024)S(1)}, f32[1280]{0:T(1024)}, u32[]{:S(2)}) copy-start(f32[1280]{0:T(1024)} %param.16) | copy-start | bytes 15364
  437.7 3.9 copy-start.3
Sparse Core Ops, SparseCore 0:
  18.4 214.0 all-gather.4
  235.1 88.5 all-gather.8
  326.5 86.6 all-gather.6
where the time goes:
time: 496 us; the launch traced here: 494 us
  waiting for transfers between devices  302 us (61%)
  local copies, waits for them, and re-layouts  67.3 us (14%)
  matrix products  45.2 us (9%)
  blocking collectives  40 us (8%)
  other arithmetic  15.7 us (3%)
  between operations  13.4 us (3%)
  starting transfers between devices  10.3 us (2%)
    all_gather x1, waiting for transfers between devices, on_device(): gathered = lax.all_gather(triple[:, :, inner:], 'patch', axis=1, tiled=True)  208 us
    all_gather x1, waiting for transfers between devices, temporal_triple(): lax.all_gather(temporal_in, 'frame', axis=0, tiled=True)  64.3 us
    all_to_all x1, blocking collectives, on_device(): lax.all_to_all(result_pos, 'frame', split_axis=0, concat_axis=1, tiled=True)  40 us
    all_gather x1, waiting for transfers between devices, temporal_project(): lax.all_gather(temporal_out, 'frame', axis=0, tiled=True)  25.6 us
    slice x2, local copies, waits for them, and re-layouts, on_device(): keys = gathered[:, :, :inner].reshape(frames, all_patches, HEADS, HDIM)  17 us
    convert_element_type x4, local copies, waits for them, and re-layouts, on_device(): moved.astype(jnp.float32) + coef_rows[:, None, None] * proj_pos  12 us
    sub x1, matrix products, on_device(): jax.nn.softmax(scores * HDIM ** (-0.5), axis=-1).astype(jnp.bfloat16)  11 us
    dot_general x2, matrix products, add_rows(): return jnp.dot(inputs, portion, preferred_element_type=jnp.float32)  10.6 us
  transfers between devices with their start and end apart: 4, of which 4 were waited for; matrix products, arithmetic and copies ran while one was open for 17% of the time, Pallas kernels for 0%

commit v1 on v0

v1 whole, which is shorter than its diff:
```python
import jax
import jax.numpy as jnp
from jax import lax
from jax.experimental import pallas as pl
from jax.experimental.pallas import tpu as pltpu
from jax.sharding import PartitionSpec as P

MESH = pl.DeviceIdType.MESH
BF = jnp.bfloat16
F32 = jnp.float32

HEADS = 8
HDIM = 80
INNER = HEADS * HDIM
D = 1280
KEEP = 0.7
EXP_SCALE = HDIM ** (-0.5) * 1.4426950408889634


def flip(a, b):
    return (a + b) % 2


def flip_x(x, key):
    low, high = x % 2, x // 2
    if key % 2:
        low = 1 - low
    if key // 2:
        high = 1 - high
    return 2 * high + low


def layer_norm(x, gain):
    center = jnp.sum(x, axis=-1, keepdims=True) * (1.0 / D)
    x = x - center
    spread = jnp.sum(x * x, axis=-1, keepdims=True) * (1.0 / D)
    return (x * lax.rsqrt(spread + 1e-06) * gain).astype(BF)


def dot(a, b):
    return jnp.dot(a, b, preferred_element_type=F32)


def dot_t(a, b):
    return lax.dot_general(a, b, (((1,), (1,)), ((), ())), preferred_element_type=F32)


def pick(rows, columns, group, stride):
    r = lax.broadcasted_iota(jnp.int32, (rows, columns), 0)
    c = lax.broadcasted_iota(jnp.int32, (rows, columns), 1)
    block = jnp.zeros_like(r)
    for n in range(1, (rows + group - 1) // group):
        block = block + (r >= n * group).astype(jnp.int32)
    hit = (c == r + block * (stride - group)) & (r < group * (columns // stride))
    return jnp.where(hit, 1.0, 0.0).astype(BF)


def layer(
    tok_hbm, swin_hbm, swout_hbm, tin_sh, tout_sh, sgain, tgain, keep, out_hbm,
    tok, swin, swout, twin, gout, twout, raw_in_st, raw_out_st, raw_in, raw_out,
    xin, q_s, k_s, v_s, o_s, mx, mback, asp, tin, tm, tb, out_v, bias,
    load_sem, tok_send, tok_recv, kv_send, kv_recv, mx_send, mx_recv,
    as_send, as_recv, tm_send, tm_recv, raw_send, raw_recv,
    ring_send, ring_recv, sib_send, sib_recv, out_sem,
):
    f = lax.axis_index("frame")
    p = lax.axis_index("patch")
    c = f % 2
    z = (f // 2) % 8
    yh = f // 16
    x = p // 2
    yl = p % 2
    fbase = f - c
    video = f // 4
    g = f % 4
    zb = z % 2
    sib = fbase + 1 - c

    def remote(src, dst, send, recv, frame, patch):
        return pltpu.make_async_remote_copy(
            src_ref=src, dst_ref=dst, send_sem=send, recv_sem=recv,
            device_id=(frame, patch), device_id_type=MESH)

    def wait_in(dst, sem):
        pltpu.make_async_copy(dst, dst, sem).wait()

    wait_out = wait_in

    loads = [
        pltpu.make_async_copy(tok_hbm, tok, load_sem.at[0]),
        pltpu.make_async_copy(swin_hbm, swin, load_sem.at[1]),
        pltpu.make_async_copy(swout_hbm, swout, load_sem.at[2]),
    ]

    barrier = pltpu.get_barrier_semaphore()

    def greet(frame, patch):
        pl.semaphore_signal(barrier, inc=1, device_id=(frame, patch), device_id_type=MESH)

    zother = (z + 7 + 2 * zb) % 8
    yflip = (f + 16) % 32 - c
    for n in range(4):
        for b in range(2):
            patch = 2 * flip_x(x, n) + flip(yl, b)
            greet(sib, patch)
            if n or b:
                greet(f, patch)
    zpair = (f - g) + 2 * (1 - zb)
    greet(zpair, p)
    greet(zpair + 1, p)
    greet(yh * 16 + 2 * zother + c, p)
    greet(yflip, 2 * x + 1 - yl)
    greet(yflip + 1, 2 * x + 1 - yl)
    loads[1].start()
    raw_in_st[...] = jnp.zeros_like(raw_in_st)
    raw_out_st[...] = jnp.zeros_like(raw_out_st)
    raw_in_st[0:40, :] = tin_sh[...]
    raw_out_st[0:20, :] = tout_sh[...]
    q_s[...] = jnp.zeros_like(q_s)
    k_s[:, 0:512, :] = jnp.zeros((HEADS, 512, 128), BF)
    lane = lax.broadcasted_iota(jnp.int32, (HEADS, 512, 128), 2)
    v_s[:, 0:512, :] = jnp.where(lane == HDIM, 1.0, 0.0).astype(BF)
    rr = lax.broadcasted_iota(jnp.int32, (256, 256), 0) % 16
    cc = lax.broadcasted_iota(jnp.int32, (256, 256), 1) % 16
    bias[...] = jnp.where(rr == cc, 0.0, -1e30).astype(F32)
    pl.semaphore_wait(barrier, 20)

    yc = flip(yl, c)
    for n in (3, 1, 2, 0):
        key = n ^ (n >> 1)
        xd = flip_x(x, key)
        for hh in (1, 0):
            half = flip(c, hh)
            src = tok_hbm.at[xd, pl.ds(4 * half, 4)]
            dst = xin.at[2 * n + yc]
            idx = 2 * n + hh
            move = remote(src, dst, tok_send.at[idx], tok_recv.at[2 * n + yc], fbase + half, 2 * xd + c)
            if n == 0 and hh == 0:
                @pl.when(yc == 0)
                def _():
                    pltpu.make_async_copy(src, dst, tok_recv.at[0]).start()

                @pl.when(yc != 0)
                def _():
                    move.start()
            else:
                move.start()

    for a, (st, raw) in enumerate(((raw_in_st, raw_in), (raw_out_st, raw_out))):
        remote(st, raw.at[c], raw_send.at[0, a], raw_recv.at[c, a], yflip + 1, 2 * x + 1 - yl).start()

        @pl.when(c == 0)
        def _():
            pltpu.make_async_copy(st, raw.at[0], raw_recv.at[0, a]).start()

        @pl.when(c != 0)
        def _():
            remote(st, raw.at[1], raw_send.at[1, a], raw_recv.at[1, a], fbase, p).start()
    loads[0].start()
    loads[2].start()

    yh_unit = flip(yh, c)
    toward = 1 - 2 * c

    def unit_at(offset):
        return yh_unit * 8 + (z + offset + 16) % 8

    def unit_refs(u):
        return (twin.at[pl.ds(pl.multiple_of(u * 80, 16), 80)], gout.at[u])

    def ring(way, step):
        sign = toward if way == 0 else -toward
        u = unit_at(-sign * (step - 1))
        frame = yh * 16 + 2 * ((z + sign + 8) % 8) + c
        return [
            remote(r, r, ring_send.at[way, step - 1, a], ring_recv.at[way, step - 1, a], frame, p)
            for a, r in enumerate(unit_refs(u))
        ]

    def ring_arrived(way, step):
        sign = toward if way == 0 else -toward
        u = unit_at(-sign * step)
        for a, r in enumerate(unit_refs(u)):
            wait_in(r, ring_recv.at[way, step - 1, a])
        return u

    def share(u, label):
        for a, r in enumerate(unit_refs(u)):
            remote(r, r, sib_send.at[label, a], sib_recv.at[label, a], sib, p).start()

    def weights_begin():
        for a, raw in enumerate((raw_in, raw_out)):
            wait_in(raw.at[0], raw_recv.at[0, a])
            wait_in(raw.at[1], raw_recv.at[1, a])
        u = unit_at(0)
        twin[pl.ds(pl.multiple_of(u * 80, 16), 80), :] = dot(
            pick(80, 96, 40, 48), raw_in[...].reshape(96, 1920)).astype(BF)
        gout[u] = dot(pick(48, 64, 20, 32), raw_out[...].reshape(64, 1280)).astype(BF)
        for way in (0, 1):
            for m in ring(way, 1):
                m.start()
        share(u, 0)

    def weights_step(step):
        for way in (0, 1):
            if way == 1 and step == 4:
                continue
            u = ring_arrived(way, step)
            if step < (4 if way == 0 else 3):
                for m in ring(way, step + 1):
                    m.start()
            share(u, step if way == 0 else 4 + step)

    def weights_end():
        weights_step(4)
        other = flip(yh_unit, 1)
        for label in range(8):
            for a, r in enumerate(unit_refs(other * 8 + label)):
                wait_in(r, sib_recv.at[label, a])
        twout[...] = dot(pick(640, 768, 40, 48), gout[...].reshape(768, 1280)).astype(BF)

    loads[1].wait()

    def chunk(n, carry):
        @pl.when(n == 1)
        def _():
            weights_begin()

        for b in range(2):
            wait_in(xin.at[2 * n + b], tok_recv.at[2 * n + b])
        rows = xin[pl.ds(2 * n, 2)].reshape(128, D).astype(F32)
        triple = dot(layer_norm(rows, sgain[...]), swin[...]).astype(BF)
        at = pl.multiple_of(n * 128, 128)
        for h in range(HEADS):
            lo = h * HDIM
            k_s[h, pl.ds(at, 128), 0:HDIM] = triple[:, INNER + lo:INNER + lo + HDIM]
            v_s[h, pl.ds(at, 128), 0:HDIM] = triple[:, 2 * INNER + lo:2 * INNER + lo + HDIM]
        for a, r in enumerate((k_s, v_s)):
            remote(r.at[:, pl.ds(at, 128)], r.at[:, pl.ds(at + 512, 128)],
                   kv_send.at[n, a], kv_recv.at[n, a], sib, p).start()
        for h in range(HEADS):
            lo = h * HDIM
            for b in range(2):
                for j in range(2):
                    at_row = (2 * b + j) * 32
                    q_s[h, j, 2 * n + b, :, 0:HDIM] = triple[at_row:at_row + 32, lo:lo + HDIM]
        return carry

    lax.fori_loop(0, 4, chunk, 0)
    for n in range(4):
        for a, r in enumerate((k_s, v_s)):
            wait_in(r.at[:, pl.ds(n * 128 + 512, 128)], kv_recv.at[n, a])

    def attend(j):
        def head(h, carry):
            q = q_s[h, j].reshape(256, 128)
            s = dot_t(q, k_s[h])
            top = jnp.max(s, axis=-1, keepdims=True)
            e = jnp.exp2((s - top) * EXP_SCALE).astype(BF)
            o = dot(e, v_s[h])
            o_s[h] = (o * (1.0 / o[:, HDIM:HDIM + 1])).astype(BF)
            return carry

        lax.fori_loop(0, HEADS, head, 0)
        mixed = jnp.concatenate([o_s[h][:, 0:HDIM] for h in range(HEADS)], axis=1)
        mx[j] = mixed.reshape(8, 2, 16, INNER)
        for s in (7, 6, 5, 4, 3, 2, 1, 0):
            n, b = s // 2, s % 2
            key = n ^ (n >> 1)
            patch = 2 * flip_x(x, key) + flip(yl, b)
            src = mx.at[j, s]
            dst = mback.at[j, pl.ds(2 * c, 2), x]
            move = remote(src, dst, mx_send.at[j, s], mx_recv.at[j, 2 * x + c], fbase + yl, patch)
            if s == 0:
                @pl.when(yc == 0)
                def _():
                    pltpu.make_async_copy(src, dst, mx_recv.at[j, 2 * x + c]).start()

                @pl.when(yc != 0)
                def _():
                    move.start()
            else:
                move.start()

    coef_space = keep[video, 0].astype(F32) / KEEP
    coef_time = keep[video, 1].astype(F32) / KEEP

    def group_of(o, j):
        return (o // 2) * 4 + j * 2 + o % 2

    def after_space(j):
        for i in range(4):
            for h in range(2):
                wait_in(mback.at[j, pl.ds(2 * h, 2), i], mx_recv.at[j, 2 * i + h])
        y = dot(mback[j].reshape(256, INNER), swout[...])
        for o in range(4):
            for i in range(4):
                at = (4 * o + i) * 16
                asp[j, o, i] = (tok[i, group_of(o, j)].astype(F32) + coef_space * y[at:at + 16]).astype(BF)
        for k in (3, 2, 1, 0):
            o = 2 * flip(g // 2, k // 2) + flip(c, k % 2)
            src, dst = asp.at[j, o], tin.at[j, g]
            if k == 0:
                pltpu.make_async_copy(src, dst, as_recv.at[j, g]).start()
            else:
                remote(src, dst, as_send.at[j, k], as_recv.at[j, g], 4 * video + o, p).start()

    def temporal(j):
        rows = tin[j].reshape(256, D).astype(F32)
        triple = dot(layer_norm(rows, tgain[...]), twin[...]).astype(BF)
        parts = []
        for h in range(HEADS):
            lo = h * HDIM
            s = dot_t(triple[:, lo:lo + HDIM], triple[:, INNER + lo:INNER + lo + HDIM]) + bias[...]
            top = jnp.max(s, axis=-1, keepdims=True)
            e = jnp.exp2((s - top) * EXP_SCALE)
            total = jnp.sum(e, axis=-1, keepdims=True)
            o = dot(e.astype(BF), triple[:, 2 * INNER + lo:2 * INNER + lo + HDIM])
            parts.append((o * (1.0 / total)).astype(BF))
        tm[j] = jnp.concatenate(parts, axis=1).reshape(4, 64, INNER)
        for k in (3, 2, 1, 0):
            o = 2 * flip(g // 2, k // 2) + flip(c, k % 2)
            src, dst = tm.at[j, o], tb.at[j, g]
            if k == 0:
                pltpu.make_async_copy(src, dst, tm_recv.at[j, g]).start()
            else:
                remote(src, dst, tm_send.at[j, k], tm_recv.at[j, g], 4 * video + o, p).start()

    def finish(j):
        for o in range(4):
            wait_in(tb.at[j, o], tm_recv.at[j, o])
        y = dot(tb[j].reshape(256, INNER), twout[...])
        for o in range(4):
            for i in range(4):
                at = (4 * o + i) * 16
                out_v[i, group_of(o, j)] = (asp[j, o, i].astype(F32) + coef_time * y[at:at + 16]).astype(BF)
        for h in range(2):
            part = pl.ds(4 * h + 2 * j, 2)
            pltpu.make_async_copy(out_v.at[:, part], out_hbm.at[:, part], out_sem.at[j, h]).start()

    weights_step(1)
    attend(0)
    weights_step(2)
    attend(1)
    loads[0].wait()
    loads[2].wait()
    after_space(0)
    weights_step(3)
    after_space(1)
    weights_end()
    for j in range(2):
        for o in range(4):
            wait_in(tin.at[j, o], as_recv.at[j, o])
        temporal(j)
    for j in range(2):
        finish(j)

    for n in range(4):
        for hh in range(2):
            part = tok_hbm.at[0, pl.ds(0, 4)]
            if n == 0 and hh == 0:
                @pl.when(yc != 0)
                def _():
                    wait_out(part, tok_send.at[0])
            else:
                wait_out(part, tok_send.at[2 * n + hh])
    for n in range(4):
        for a, r in enumerate((k_s, v_s)):
            wait_out(r.at[:, pl.ds(n * 128, 128)], kv_send.at[n, a])
    for j in range(2):
        for s in range(8):
            if s == 0:
                @pl.when(yc != 0)
                def _():
                    wait_out(mx.at[j, s], mx_send.at[j, s])
            else:
                wait_out(mx.at[j, s], mx_send.at[j, s])
        for k in range(1, 4):
            wait_out(asp.at[j, k], as_send.at[j, k])
            wait_out(tm.at[j, k], tm_send.at[j, k])
    for a, st in enumerate((raw_in_st, raw_out_st)):
        wait_out(st, raw_send.at[0, a])

        @pl.when(c != 0)
        def _():
            wait_out(st, raw_send.at[1, a])
    for a, r in enumerate(unit_refs(0)):
        for way in range(2):
            for step in range(4 - way):
                wait_out(r, ring_send.at[way, step, a])
        for label in range(8):
            wait_out(r, sib_send.at[label, a])
    for j in range(2):
        for h in range(2):
            part = pl.ds(4 * h + 2 * j, 2)
            pltpu.make_async_copy(out_v.at[:, part], out_hbm.at[:, part], out_sem.at[j, h]).wait()


def on_device(tokens, spatial_in, spatial_out, temporal_in, temporal_out, spatial_gain, temporal_gain, keep_masks):
    dma = pltpu.SemaphoreType.DMA
    scratch = [
        pltpu.VMEM((4, 8, 16, D), BF),
        pltpu.VMEM((D, 3 * INNER), BF),
        pltpu.VMEM((INNER, D), BF),
        pltpu.VMEM((D, 3 * INNER), BF),
        pltpu.VMEM((16, 48, D), BF),
        pltpu.VMEM((INNER, D), BF),
        pltpu.VMEM((48, 3 * INNER), BF),
        pltpu.VMEM((32, D), BF),
        pltpu.VMEM((2, 48, 3 * INNER), BF),
        pltpu.VMEM((2, 32, D), BF),
        pltpu.VMEM((8, 4, 16, D), BF),
        pltpu.VMEM((HEADS, 2, 8, 32, 128), BF),
        pltpu.VMEM((HEADS, 1024, 128), BF),
        pltpu.VMEM((HEADS, 1024, 128), BF),
        pltpu.VMEM((HEADS, 256, 128), BF),
        pltpu.VMEM((2, 8, 2, 16, INNER), BF),
        pltpu.VMEM((2, 4, 4, 16, INNER), BF),
        pltpu.VMEM((2, 4, 4, 16, D), BF),
        pltpu.VMEM((2, 4, 4, 16, D), BF),
        pltpu.VMEM((2, 4, 64, INNER), BF),
        pltpu.VMEM((2, 4, 64, INNER), BF),
        pltpu.VMEM((4, 8, 16, D), BF),
        pltpu.VMEM((256, 256), F32),
        dma((3,)), dma((8,)), dma((8,)), dma((4, 2)), dma((4, 2)), dma((2, 8)), dma((2, 8)),
        dma((2, 4)), dma((2, 4)), dma((2, 4)), dma((2, 4)), dma((2, 2)), dma((2, 2)),
        dma((2, 4, 2)), dma((2, 4, 2)), dma((8, 2)), dma((8, 2)), dma((2, 2)),
    ]
    any_space = pl.BlockSpec(memory_space=pl.ANY)
    vmem = pl.BlockSpec(memory_space=pltpu.VMEM)
    out = pl.pallas_call(
        layer,
        out_shape=jax.ShapeDtypeStruct((4, 8, 16, D), BF),
        in_specs=[any_space, any_space, any_space, vmem, vmem, vmem, vmem,
                  pl.BlockSpec(memory_space=pltpu.SMEM)],
        out_specs=any_space,
        scratch_shapes=scratch,
        compiler_params=pltpu.CompilerParams(
            collective_id=0, has_side_effects=True, vmem_limit_bytes=60 * 1024 * 1024),
    )(tokens.reshape(4, 8, 16, D), spatial_in, spatial_out, temporal_in, temporal_out,
      spatial_gain.reshape(1, D), temporal_gain.reshape(1, D), keep_masks)
    return out.reshape(4, 128, D)


def solution(mesh):
    placed = (
        P("frame", "patch", None), P(), P(), P("frame", None), P("frame", None), P(), P(), P(),
    )
    return jax.shard_map(
        on_device, mesh=mesh, in_specs=placed, out_specs=P("frame", "patch", None), check_vma=False)
```

time: 496 us -> 94.3 us (0.19)
  waiting for transfers between devices: 302 us -> 0 us
  Pallas kernels: 0 us -> 87.6 us
  local copies, waits for them, and re-layouts: 67.3 us -> 6.38 us
  matrix products: 45.2 us -> 0 us
  blocking collectives: 40 us -> 0 us
  other arithmetic: 15.7 us -> 0 us
  between operations: 13.4 us -> 0.01 us
  starting transfers between devices: 10.3 us -> 0 us
    all_gather x3 -> x0, waiting for transfers between devices: 298 us -> none  [the longest x1 208 us: on_device(): gathered = lax.all_gather(triple[:, :, inner:], 'patch', axis=1, tiled=True)]
    pallas_call x0 -> x1, Pallas kernels: none -> 87.6 us  [on_device(): pl.pallas_call(layer, out_shape=jax.ShapeDtypeStruct((4, 8, 16, D), BF),...]
    all_to_all x1 -> x0, blocking collectives: 40 us -> none  [on_device(): lax.all_to_all(result_pos, 'frame', split_axis=0, concat_axis=1, tiled=True)]
    slice x7 -> x0, local copies, waits for them, and re-layouts: 34.3 us -> none  [the longest x2 17 us: on_device(): keys = gathered[:, :, :inner].reshape(frames, all_patches, HEADS, HDIM)]
    dot_general x6 -> x0, matrix products: 29.8 us -> none  [the longest x2 10.6 us: add_rows(): return jnp.dot(inputs, portion, preferred_element_type=jnp.float32)]
    convert_element_type x7 -> x0, local copies, waits for them, and re-layouts: 16.4 us -> none  [the longest x4 12 us: on_device(): moved.astype(jnp.float32) + coef_rows[:, None, None] * proj_pos]
    sub x2 -> x0, matrix products: 15.3 us -> none  [the longest x1 11 us: on_device(): jax.nn.softmax(scores * HDIM ** (-0.5), axis=-1).astype(jnp.bfloat16)]
    all_to_all x1 -> x0, starting transfers between devices: 10 us -> none  [on_device(): lax.all_to_all(after_space, 'frame', split_axis=1, concat_axis=0, tiled=T...]
  transfers between devices with their start and end apart: 4 -> 0, of which waited for: 4 -> 0; matrix products, arithmetic and copies ran while one was open for 17% -> 0% of each run, Pallas kernels for 0% -> 0%
where the time goes in v1:
time: 94.3 us; the launch traced here: 94 us
  Pallas kernels  87.6 us (93%)
  local copies, waits for them, and re-layouts  6.38 us (7%)
    pallas_call x1, Pallas kernels, on_device(): pl.pallas_call(layer, out_shape=jax.ShapeDtypeStruct((4, 8, 16, D), BF),...  87.6 us
    unnamed x2, local copies, waits for them, and re-layouts  3.8 us

profile of v1, /device:TPU:1, one launch (start us, length us, event | category | flops | bytes accessed | tf_op | source)
XLA Modules:
  0.0 94.0 jit_solution(15440452039575418341)
XLA Ops:
  0.0 1.3 %copy.9.keep = s32[8,2]{1,0:T(8,128)} copy(s32[8,2]{0,1:T(2,128)} %param.15) | data formatting | bytes 128 | tf_op args[7]
  1.3 1.3 %reshape.13.sgain = f32[1,1280]{1,0:T(1,128)} reshape(f32[1280]{0:T(1024)} %param.13) | data formatting | bytes 10240 | tf_op jit(solution)/shard_map/reshape | solution.py:441
  2.6 1.3 %reshape.14.tgain = f32[1,1280]{1,0:T(1,128)} reshape(f32[1280]{0:T(1024)} %param.14) | data formatting | bytes 10240 | tf_op jit(solution)/shard_map/reshape | solution.py:441
  3.9 87.6 %shard_map.82 = bf16[4,8,16,1280]{3,2,1,0:T(8,128)(2,1)} custom-call(bf16[4,8,16,1280]{3,2,1,0:T(8,128)(2,1)} %bitcast.3, bf16[1280,1920]{1,0:T(8,128)(2,1)} %swin_hbm.1, bf16[640,1280]{1,0:T(8,128)(2,1)} %swout_hbm.1, bf16[40,1920]{1,0:T(8,128)(2,1)} %tin_sh.1, bf16[20,1280]{1,0:T(8,128)(2,1)} %tout_sh.1, f32[1,1280]{1,0:T(1,128)} %reshape.13.sgain, ...), custom_call_target="tpu_custom_call" | custom-call | tf_op jit(solution)/shard_map/pallas_call | solution.py:431
  91.5 2.5 %copy.11 = bf16[4,128,1280]{2,1,0:T(8,128)(2,1)} copy(bf16[4,128,1280]{2,1,0:T(8,128)(2,1)} %bitcast.2) | data formatting | bytes 2621440

commit v2 on v1

v2 whole, which is shorter than its diff:
```python
import jax
import jax.numpy as jnp
from jax import lax
from jax.experimental import pallas as pl
from jax.experimental.pallas import tpu as pltpu
from jax.sharding import PartitionSpec as P

MESH = pl.DeviceIdType.MESH
BF = jnp.bfloat16
F32 = jnp.float32

HEADS = 8
HDIM = 80
INNER = HEADS * HDIM
D = 1280
KEEP = 0.7
UNROLL = 4
SERVICE = ((0, ((0, 1), (1, 1)), ()), (2, ((0, 2), (1, 2)), (0,)))
PLAN = (
    ('attend', 0, 1),
    ('core1', 1),
    ('core0', (0, 3), (1, 3)),
    ('attend', 1, 1),
    ('after', 0),
    ('core1', 2),
    ('attend', 2, 1),
    ('after', 1),
    ('core0', (0, 4)),
    ('attend', 3, 1),
    ('core1', 3),
    ('after', 2),
    ('after', 3),
    ('end',),
    ('temporal', 0, 2),
    ('temporal', 2, 2),
    ('finish', 0, 2),
    ('finish', 2, 2),
)
EXP_SCALE = HDIM ** (-0.5) * 1.4426950408889634


def flip(a, b):
    return (a + b) % 2


def flip_x(x, key):
    low, high = x % 2, x // 2
    if key % 2:
        low = 1 - low
    if key // 2:
        high = 1 - high
    return 2 * high + low


def layer_norm(x, gain):
    center = jnp.sum(x, axis=-1, keepdims=True) * (1.0 / D)
    x = x - center
    spread = jnp.sum(x * x, axis=-1, keepdims=True) * (1.0 / D)
    return (x * lax.rsqrt(spread + 1e-06) * gain).astype(BF)


def dot(a, b):
    return jnp.dot(a, b, preferred_element_type=F32)


def dot_t(a, b):
    return lax.dot_general(a, b, (((1,), (1,)), ((), ())), preferred_element_type=F32)


def pick(rows, columns, group, stride):
    r = lax.broadcasted_iota(jnp.int32, (rows, columns), 0)
    c = lax.broadcasted_iota(jnp.int32, (rows, columns), 1)
    block = jnp.zeros_like(r)
    for n in range(1, (rows + group - 1) // group):
        block = block + (r >= n * group).astype(jnp.int32)
    hit = (c == r + block * (stride - group)) & (r < group * (columns // stride))
    return jnp.where(hit, 1.0, 0.0).astype(BF)


def layer(
    tok_hbm, swin_hbm, swout_hbm, tin_sh, tout_sh, sgain, tgain, keep, out_hbm,
    tok, swin, swout, twin, gout, twout, raw_in_st, raw_out_st, raw_in, raw_out,
    xin, q_s, k_s, v_s, o_s, mx, mback, asp, tin, tm, tb, out_v, bias,
    load_sem, tok_send, tok_recv, kv_send, kv_recv, mx_send, mx_recv,
    as_send, as_recv, tm_send, tm_recv, raw_send, raw_recv,
    ring_send, ring_recv, sib_send, sib_recv, lend_send, lend_recv, out_sem,
):
    f = lax.axis_index("frame")
    p = lax.axis_index("patch")
    c = f % 2
    z = (f // 2) % 8
    yh = f // 16
    x = p // 2
    yl = p % 2
    fbase = f - c
    video = f // 4
    g = f % 4
    zb = z % 2
    sib = fbase + 1 - c

    def remote(src, dst, send, recv, frame, patch):
        return pltpu.make_async_remote_copy(
            src_ref=src, dst_ref=dst, send_sem=send, recv_sem=recv,
            device_id=(frame, patch), device_id_type=MESH)

    def wait_in(dst, sem):
        pltpu.make_async_copy(dst, dst, sem).wait()

    wait_out = wait_in

    loads = [
        pltpu.make_async_copy(tok_hbm, tok, load_sem.at[0]),
        pltpu.make_async_copy(swin_hbm, swin, load_sem.at[1]),
        pltpu.make_async_copy(swout_hbm, swout, load_sem.at[2]),
    ]

    barrier = pltpu.get_barrier_semaphore()

    def greet(frame, patch):
        pl.semaphore_signal(barrier, inc=1, device_id=(frame, patch), device_id_type=MESH)

    zother = (z + 7 + 2 * zb) % 8
    yflip = (f + 16) % 32 - c
    for n in range(4):
        for b in range(2):
            patch = 2 * flip_x(x, n) + flip(yl, b)
            greet(sib, patch)
            if n or b:
                greet(f, patch)
    zpair = (f - g) + 2 * (1 - zb)
    greet(zpair, p)
    greet(zpair + 1, p)
    greet(yh * 16 + 2 * zother + c, p)
    greet(yflip, 2 * x + 1 - yl)
    greet(yflip + 1, 2 * x + 1 - yl)
    loads[1].start()
    raw_in_st[...] = jnp.zeros_like(raw_in_st)
    raw_out_st[...] = jnp.zeros_like(raw_out_st)
    raw_in_st[0:40, :] = tin_sh[...]
    raw_out_st[0:20, :] = tout_sh[...]
    pl.semaphore_wait(barrier, 20)

    for a, (st, raw) in enumerate(((raw_in_st, raw_in), (raw_out_st, raw_out))):
        remote(st, raw.at[c], raw_send.at[0, a], raw_recv.at[c, a], yflip + 1, 2 * x + 1 - yl).start()

        @pl.when(c == 0)
        def _():
            pltpu.make_async_copy(st, raw.at[0], raw_recv.at[0, a]).start()

        @pl.when(c != 0)
        def _():
            remote(st, raw.at[1], raw_send.at[1, a], raw_recv.at[1, a], fbase, p).start()
    yc = flip(yl, c)

    def send_wave(w):
        for n in range(4):
            xd = flip_x(x, n ^ (n >> 1))
            for hh in (1, 0):
                half = flip(c, hh)
                src = tok_hbm.at[xd, 4 * half + w]
                dst = xin.at[w, 2 * n + yc]
                arrive = tok_recv.at[w, 2 * n + yc]
                move = remote(src, dst, tok_send.at[w, 2 * n + hh], arrive, fbase + half, 2 * xd + c)
                if n == 0 and hh == 0:
                    @pl.when(yc == 0)
                    def _():
                        pltpu.make_async_copy(src, dst, arrive).start()

                    @pl.when(yc != 0)
                    def _():
                        move.start()
                else:
                    move.start()

    for w in range(4):
        send_wave(w)
    loads[0].start()
    loads[2].start()

    q_s[...] = jnp.zeros_like(q_s)
    k_s[0:4, :, HDIM:, :] = jnp.zeros((4, HEADS, 128 - HDIM, 128), BF)
    lane = lax.broadcasted_iota(jnp.int32, (128, 128), 1)
    ones = jnp.where(lane == HDIM, 1.0, 0.0).astype(BF)
    v_s[0:4] = jnp.broadcast_to(ones, (4, HEADS, 128, 128))
    rr = lax.broadcasted_iota(jnp.int32, (256, 256), 0)
    cc = lax.broadcasted_iota(jnp.int32, (256, 256), 1)
    bias[...] = jnp.where((rr % 8 == cc % 8) & (rr // 128 == cc // 128), 0.0, -1e30).astype(F32)

    yh_unit = flip(yh, c)
    toward = 1 - 2 * c

    def unit_at(offset):
        return yh_unit * 8 + (z + offset + 16) % 8

    def unit_refs(u):
        return (twin.at[pl.ds(pl.multiple_of(u * 80, 16), 80)], gout.at[u])

    lent = ((0, 1), (1, 1), (0, 2), (1, 2), (0, 4))

    def way_sign(way):
        return toward if way == 0 else -toward

    def ring(way, step):
        sign = way_sign(way)
        u = unit_at(-sign * (step - 1))
        frame = yh * 16 + 2 * ((z + sign + 8) % 8) + c
        return [
            remote(r, r, ring_send.at[way, step - 1, a], ring_recv.at[way, step - 1, a], frame, p)
            for a, r in enumerate(unit_refs(u))
        ]

    def ring_arrived(way, step):
        u = unit_at(-way_sign(way) * step)
        for a, r in enumerate(unit_refs(u)):
            wait_in(r, ring_recv.at[way, step - 1, a])
        return u

    def share(u, label):
        for a, r in enumerate(unit_refs(u)):
            remote(r, r, sib_send.at[label, a], sib_recv.at[label, a], sib, p).start()

    def weights_begin():
        for a, raw in enumerate((raw_in, raw_out)):
            wait_in(raw.at[0], raw_recv.at[0, a])
            wait_in(raw.at[1], raw_recv.at[1, a])
        u = unit_at(0)
        twin[pl.ds(pl.multiple_of(u * 80, 16), 80), :] = dot(
            pick(80, 96, 40, 48), raw_in[...].reshape(96, 1920)).astype(BF)
        gout[u] = dot(pick(48, 64, 20, 32), raw_out[...].reshape(64, 1280)).astype(BF)

        @pl.when(c == 0)
        def _():
            for way in (0, 1):
                for m in ring(way, 1):
                    m.start()

        share(u, 0)

    def weights_pass(way, step):
        u = ring_arrived(way, step)
        if step < 4 - way:
            for m in ring(way, step + 1):
                m.start()
        if (way, step) in lent:
            label = lent.index((way, step))
            for a, r in enumerate(unit_refs(u)):
                remote(r, r, lend_send.at[label, a], lend_recv.at[label, a], yflip + 1, 2 * x + 1 - yl).start()
        share(u, step if way == 0 else 4 + step)

    def weights_lent(label):
        way, step = lent[label]
        u = unit_at(-step if way == 0 else step)
        for a, r in enumerate(unit_refs(u)):
            wait_in(r, lend_recv.at[label, a])
        if step == 2:
            for m in ring(1 - way, 3):
                m.start()
        share(u, 8 + label)

    def core0(*moves):
        @pl.when(c == 0)
        def _():
            for way, step in moves:
                weights_pass(way, step)

    def core1(*moves):
        @pl.when(c == 1)
        def _():
            for label in moves:
                weights_lent(label)

    def labels(core):
        return [0, 1, 2, 3, 4, 5, 6, 7] if core == 0 else [0, 3, 7, 8, 9, 10, 11, 12]

    def weights_end():
        @pl.when(c == 1)
        def _():
            for way in (0, 1):
                share(ring_arrived(way, 3), 3 + 4 * way)
            weights_lent(4)

        other = flip(yh_unit, 1)
        for core in (0, 1):
            @pl.when(c != core)
            def _():
                for n, label in enumerate(labels(core)):
                    for a, r in enumerate(unit_refs(other * 8 + n)):
                        wait_in(r, sib_recv.at[label, a])
        twout[...] = dot(pick(640, 768, 40, 48), gout[...].reshape(768, 1280)).astype(BF)

    weights_begin()
    loads[1].wait()

    def chunk(w, carry):
        for s in range(8):
            wait_in(xin.at[w, s], tok_recv.at[w, s])
        rows = xin[w].reshape(128, D).astype(F32)
        normed = layer_norm(rows, sgain[...].reshape(1, D))
        pair = dot(normed, swin[:, INNER:]).astype(BF)
        keys = pair[:, 0:INNER].T
        for h in range(HEADS):
            lo = h * HDIM
            k_s[w, h, 0:HDIM, :] = keys[lo:lo + HDIM]
            v_s[w, h, :, 0:HDIM] = pair[:, INNER + lo:INNER + lo + HDIM]
        for a, r in enumerate((k_s, v_s)):
            remote(r.at[w], r.at[w + 4], kv_send.at[w, a], kv_recv.at[w, a], sib, p).start()
        queries = dot(normed, swin[:, 0:INNER]).astype(BF)
        for h in range(HEADS):
            q_s[h, w, :, 0:HDIM] = queries[:, h * HDIM:(h + 1) * HDIM]
        for after, moves0, moves1 in SERVICE:
            @pl.when(w == after)
            def _():
                core0(*moves0)
                core1(*moves1)

        return carry

    lax.fori_loop(0, 4, chunk, 0)
    for n in range(4):
        for a, r in enumerate((k_s, v_s)):
            wait_in(r.at[n + 4], kv_recv.at[n, a])

    def attend(w, count, first=0, last=HEADS):
        def head(h, carry):
            q = q_s[h, w:w + count].reshape(count * 128, 128)
            s = dot(q, jnp.concatenate([k_s[n, h] for n in range(8)], axis=1))
            top = jnp.max(s, axis=-1, keepdims=True)
            e = jnp.exp2((s - top) * EXP_SCALE).astype(BF)
            o = dot(e, v_s[:, h].reshape(1024, 128))
            o_s[h, 0:count * 128] = (o * (1.0 / o[:, HDIM:HDIM + 1])).astype(BF)
            return carry

        lax.fori_loop(first, last, head, 0, unroll=UNROLL)
        if last < HEADS:
            return
        mixed = jnp.concatenate([o_s[h, 0:count * 128, 0:HDIM] for h in range(HEADS)], axis=1)
        mx[w:w + count] = mixed.reshape(count, 8, 16, INNER)
        for v in range(w, w + count):
            for s in (7, 6, 5, 4, 3, 2, 1, 0):
                n, b = s // 2, s % 2
                patch = 2 * flip_x(x, n ^ (n >> 1)) + flip(yl, b)
                src, dst, arrive = mx.at[v, s], mback.at[v, c, x], mx_recv.at[v, c, x]
                move = remote(src, dst, mx_send.at[v, s], arrive, fbase + yl, patch)
                if s == 0:
                    @pl.when(yc == 0)
                    def _():
                        pltpu.make_async_copy(src, dst, arrive).start()

                    @pl.when(yc != 0)
                    def _():
                        move.start()
                else:
                    move.start()

    coef_space = keep[0, video].astype(F32) / KEEP
    coef_time = keep[1, video].astype(F32) / KEEP

    def to_video(w, src_buf, dst_buf, send, arrive):
        for k in (3, 2, 1, 0):
            o = 2 * flip(g // 2, k // 2) + flip(c, k % 2)
            src, dst = src_buf.at[w, o], dst_buf.at[w, g]
            if k == 0:
                pltpu.make_async_copy(src, dst, arrive.at[w, g]).start()
            else:
                remote(src, dst, send.at[w, k], arrive.at[w, g], 4 * video + o, p).start()

    def after_space(w):
        for h in range(2):
            for i in range(4):
                wait_in(mback.at[w, h, i], mx_recv.at[w, h, i])
        y = dot(mback[w].reshape(128, INNER), swout[...]) * coef_space
        for h in range(2):
            rows = [tok[i, 4 * h + w].astype(F32) + y[(4 * h + i) * 16:(4 * h + i + 1) * 16] for i in range(4)]
            for core in range(2):
                asp[w, 2 * h + core] = jnp.concatenate([r[8 * core:8 * core + 8] for r in rows], axis=0).astype(BF)
        to_video(w, asp, tin, as_send, as_recv)

    def temporal(w, count):
        for v in range(w, w + count):
            for o in range(4):
                wait_in(tin.at[v, o], as_recv.at[v, o])
        size = count * 128
        rows = tin[w:w + count].reshape(size, D).astype(F32)
        triple = dot(layer_norm(rows, tgain[...].reshape(1, D)), twin[...]).astype(BF)
        parts = []
        for h in range(HEADS):
            lo = h * HDIM
            s = dot_t(triple[:, lo:lo + HDIM], triple[:, INNER + lo:INNER + lo + HDIM]) + bias[0:size, 0:size]
            top = jnp.max(s, axis=-1, keepdims=True)
            e = jnp.exp2((s - top) * EXP_SCALE)
            total = jnp.sum(e, axis=-1, keepdims=True)
            o = dot(e.astype(BF), triple[:, 2 * INNER + lo:2 * INNER + lo + HDIM])
            parts.append((o * (1.0 / total)).astype(BF))
        tm[w:w + count] = jnp.concatenate(parts, axis=1).reshape(count, 4, 32, INNER)
        for v in range(w, w + count):
            to_video(v, tm, tb, tm_send, tm_recv)

    def finish(w, count):
        for v in range(w, w + count):
            for o in range(4):
                wait_in(tb.at[v, o], tm_recv.at[v, o])
        y = dot(tb[w:w + count].reshape(count * 128, INNER), twout[...]) * coef_time
        for v in range(w, w + count):
            for h in range(2):
                low, high = [
                    asp[v, 2 * h + core].astype(F32)
                    + y[((v - w) * 4 + 2 * h + core) * 32:((v - w) * 4 + 2 * h + core + 1) * 32]
                    for core in range(2)]
                for i in range(4):
                    out_v[i, 4 * h + v] = jnp.concatenate(
                        [low[8 * i:8 * i + 8], high[8 * i:8 * i + 8]], axis=0).astype(BF)
            for h in range(2):
                pltpu.make_async_copy(out_v.at[:, 4 * h + v], out_hbm.at[:, 4 * h + v], out_sem.at[v, h]).start()

    loads[0].wait()
    loads[2].wait()
    for move, *what in PLAN:
        {'attend': attend, 'after': after_space, 'temporal': temporal, 'finish': finish,
         'core0': core0, 'core1': core1, 'end': weights_end}[move](*what)

    for w in range(4):
        part = tok_hbm.at[0, 0]
        for s in range(8):
            if s == 0:
                @pl.when(yc != 0)
                def _():
                    wait_out(part, tok_send.at[w, 0])
                    wait_out(mx.at[w, 0], mx_send.at[w, 0])
            else:
                wait_out(part, tok_send.at[w, s])
                wait_out(mx.at[w, s], mx_send.at[w, s])
        for a, r in enumerate((k_s, v_s)):
            wait_out(r.at[w], kv_send.at[w, a])
        for k in range(1, 4):
            wait_out(asp.at[w, k], as_send.at[w, k])
            wait_out(tm.at[w, k], tm_send.at[w, k])
    for a, st in enumerate((raw_in_st, raw_out_st)):
        wait_out(st, raw_send.at[0, a])

        @pl.when(c != 0)
        def _():
            wait_out(st, raw_send.at[1, a])
    for a, r in enumerate(unit_refs(0)):
        for core in (0, 1):
            @pl.when(c == core)
            def _():
                for way in range(2):
                    for step in (range(4 - way) if core == 0 else (2,)):
                        wait_out(r, ring_send.at[way, step, a])
                for label in labels(core):
                    wait_out(r, sib_send.at[label, a])
                if core == 0:
                    for label in range(len(lent)):
                        wait_out(r, lend_send.at[label, a])
    for w in range(4):
        for h in range(2):
            pltpu.make_async_copy(out_v.at[:, 4 * h + w], out_hbm.at[:, 4 * h + w], out_sem.at[w, h]).wait()


def on_device(tokens, spatial_in, spatial_out, temporal_in, temporal_out, spatial_gain, temporal_gain, keep_masks):
    dma = pltpu.SemaphoreType.DMA
    scratch = [
        pltpu.VMEM((4, 8, 16, D), BF),
        pltpu.VMEM((D, 3 * INNER), BF),
        pltpu.VMEM((INNER, D), BF),
        pltpu.VMEM((D, 3 * INNER), BF),
        pltpu.VMEM((16, 48, D), BF),
        pltpu.VMEM((INNER, D), BF),
        pltpu.VMEM((48, 3 * INNER), BF),
        pltpu.VMEM((32, D), BF),
        pltpu.VMEM((2, 48, 3 * INNER), BF),
        pltpu.VMEM((2, 32, D), BF),
        pltpu.VMEM((4, 8, 16, D), BF),
        pltpu.VMEM((HEADS, 4, 128, 128), BF),
        pltpu.VMEM((8, HEADS, 128, 128), BF),
        pltpu.VMEM((8, HEADS, 128, 128), BF),
        pltpu.VMEM((HEADS, 256, 128), BF),
        pltpu.VMEM((4, 8, 16, INNER), BF),
        pltpu.VMEM((4, 2, 4, 16, INNER), BF),
        pltpu.VMEM((4, 4, 32, D), BF),
        pltpu.VMEM((4, 4, 32, D), BF),
        pltpu.VMEM((4, 4, 32, INNER), BF),
        pltpu.VMEM((4, 4, 32, INNER), BF),
        pltpu.VMEM((4, 8, 16, D), BF),
        pltpu.VMEM((256, 256), F32),
        dma((3,)), dma((4, 8)), dma((4, 8)), dma((4, 2)), dma((4, 2)), dma((4, 8)), dma((4, 2, 4)),
        dma((4, 4)), dma((4, 4)), dma((4, 4)), dma((4, 4)), dma((2, 2)), dma((2, 2)),
        dma((2, 4, 2)), dma((2, 4, 2)), dma((13, 2)), dma((13, 2)), dma((5, 2)), dma((5, 2)), dma((4, 2)),
    ]
    any_space = pl.BlockSpec(memory_space=pl.ANY)
    vmem = pl.BlockSpec(memory_space=pltpu.VMEM)
    out = pl.pallas_call(
        layer,
        out_shape=jax.ShapeDtypeStruct((4, 8, 16, D), BF),
        in_specs=[any_space, any_space, any_space, vmem, vmem, vmem, vmem,
                  pl.BlockSpec(memory_space=pltpu.SMEM)],
        out_specs=any_space,
        scratch_shapes=scratch,
        compiler_params=pltpu.CompilerParams(
            collective_id=0, has_side_effects=True, vmem_limit_bytes=60 * 1024 * 1024),
    )(tokens.reshape(4, 8, 16, D), spatial_in, spatial_out, temporal_in, temporal_out,
      spatial_gain, temporal_gain, keep_masks.T)
    return out.reshape(4, 128, D)


def solution(mesh):
    placed = (
        P("frame", "patch", None), P(), P(), P("frame", None), P("frame", None), P(), P(), P(),
    )
    return jax.shard_map(
        on_device, mesh=mesh, in_specs=placed, out_specs=P("frame", "patch", None), check_vma=False)
```

time: 94.3 us -> 75.9 us (0.80)
  Pallas kernels: 87.6 us -> 73.3 us
  local copies, waits for them, and re-layouts: 6.38 us -> 2.46 us
    pallas_call x1, Pallas kernels: 87.6 us -> 73.3 us  [on_device(): pl.pallas_call(layer, out_shape=jax.ShapeDtypeStruct((4, 8, 16, D), BF),...]
    reshape x2 -> x0, local copies, waits for them, and re-layouts: 2.58 us -> none  [the longest x1 1.29 us: on_device(): spatial_gain.reshape(1, D)]
    unnamed x2 -> x1, local copies, waits for them, and re-layouts: 3.8 us -> 2.46 us
where the time goes in v2:
time: 75.9 us; the launch traced here: 75.7 us
  Pallas kernels  73.3 us (97%)
  local copies, waits for them, and re-layouts  2.46 us (3%)
    pallas_call x1, Pallas kernels, on_device(): pl.pallas_call(layer, out_shape=jax.ShapeDtypeStruct((4, 8, 16, D), BF),...  73.3 us
    unnamed x1, local copies, waits for them, and re-layouts  2.46 us

profile of v2, /device:TPU:1, one launch (start us, length us, event | category | flops | bytes accessed | tf_op | source)
XLA Modules:
  0.0 75.7 jit_solution(401859637167919639)
XLA Ops:
  0.0 73.3 %shard_map.82 = bf16[4,8,16,1280]{3,2,1,0:T(8,128)(2,1)} custom-call(bf16[4,8,16,1280]{3,2,1,0:T(8,128)(2,1)} %bitcast.4, bf16[1280,1920]{1,0:T(8,128)(2,1)} %swin_hbm.1, bf16[640,1280]{1,0:T(8,128)(2,1)} %swout_hbm.1, bf16[40,1920]{1,0:T(8,128)(2,1)} %tin_sh.1, bf16[20,1280]{1,0:T(8,128)(2,1)} %tout_sh.1, f32[1280]{0:T(1024)} %sgain.1, f32[1280]{0:T(1024)} %tgain.1, ...), custom_call_target="tpu_custom_call" | custom-call | tf_op jit(solution)/shard_map/pallas_call | solution.py:492
  73.3 2.5 %copy.10 = bf16[4,128,1280]{2,1,0:T(8,128)(2,1)} copy(bf16[4,128,1280]{2,1,0:T(8,128)(2,1)} %bitcast.3) | data formatting | bytes 2621440

commit v3 on v2

--- a/solution.py
+++ b/solution.py
@@ -15,24 +15,25 @@
 D = 1280
 KEEP = 0.7
 UNROLL = 4
-SERVICE = ((0, ((0, 1), (1, 1)), ()), (2, ((0, 2), (1, 2)), (0,)))
+SERVICE = ((0, ((0, 1), (1, 1)), ()), (2, ((0, 2), (1, 2)), ((1, True),)))
 PLAN = (
     ('attend', 0, 1),
-    ('core1', 1),
     ('core0', (0, 3), (1, 3)),
+    ('core1', (1, False), (2, True)),
     ('attend', 1, 1),
     ('after', 0),
-    ('core1', 2),
     ('attend', 2, 1),
     ('after', 1),
     ('core0', (0, 4)),
+    ('core1', (2, False), (3, True)),
     ('attend', 3, 1),
-    ('core1', 3),
     ('after', 2),
     ('after', 3),
+    ('core1', (3, False)),
     ('end',),
     ('temporal', 0, 2),
     ('temporal', 2, 2),
+    ('out',),
     ('finish', 0, 2),
     ('finish', 2, 2),
 )
@@ -195,7 +196,7 @@
     def unit_refs(u):
         return (twin.at[pl.ds(pl.multiple_of(u * 80, 16), 80)], gout.at[u])
 
-    lent = ((0, 1), (1, 1), (0, 2), (1, 2), (0, 4))
+    odd = x % 2
 
     def way_sign(way):
         return toward if way == 0 else -toward
@@ -241,20 +242,23 @@
         if step < 4 - way:
             for m in ring(way, step + 1):
                 m.start()
-        if (way, step) in lent:
-            label = lent.index((way, step))
+        label = 2 * (step - 1) + way
+
+        @pl.when((odd == way) | (step == 4))
+        def _():
             for a, r in enumerate(unit_refs(u)):
                 remote(r, r, lend_send.at[label, a], lend_recv.at[label, a], yflip + 1, 2 * x + 1 - yl).start()
+
         share(u, step if way == 0 else 4 + step)
 
-    def weights_lent(label):
-        way, step = lent[label]
-        u = unit_at(-step if way == 0 else step)
+    def weights_lent(step, direct):
+        way = odd if direct else 1 - odd
+        u = unit_at(step * (2 * way - 1))
+        label = 2 * (step - 1) + way
         for a, r in enumerate(unit_refs(u)):
             wait_in(r, lend_recv.at[label, a])
-        if step == 2:
-            for m in ring(1 - way, 3):
-                m.start()
+            if direct:
+                remote(r, r, lend_send.at[label, a], lend_recv.at[label, a], f, 2 * flip_x(x, 1) + yl).start()
         share(u, 8 + label)
 
     def core0(*moves):
@@ -266,18 +270,19 @@
     def core1(*moves):
         @pl.when(c == 1)
         def _():
-            for label in moves:
-                weights_lent(label)
+            for move in moves:
+                weights_lent(*move)
 
     def labels(core):
-        return [0, 1, 2, 3, 4, 5, 6, 7] if core == 0 else [0, 3, 7, 8, 9, 10, 11, 12]
+        return [0, 1, 2, 3, 4, 5, 6, 7] if core == 0 else [0, 8, 9, 10, 11, 12, 13, 14]
 
     def weights_end():
         @pl.when(c == 1)
         def _():
-            for way in (0, 1):
-                share(ring_arrived(way, 3), 3 + 4 * way)
-            weights_lent(4)
+            u = unit_at(4)
+            for a, r in enumerate(unit_refs(u)):
+                wait_in(r, lend_recv.at[6, a])
+            share(u, 14)
 
         other = flip(yh_unit, 1)
         for core in (0, 1):
@@ -286,6 +291,8 @@
                 for n, label in enumerate(labels(core)):
                     for a, r in enumerate(unit_refs(other * 8 + n)):
                         wait_in(r, sib_recv.at[label, a])
+
+    def weights_out():
         twout[...] = dot(pick(640, 768, 40, 48), gout[...].reshape(768, 1280)).astype(BF)
 
     weights_begin()
@@ -416,7 +423,8 @@
     loads[2].wait()
     for move, *what in PLAN:
         {'attend': attend, 'after': after_space, 'temporal': temporal, 'finish': finish,
-         'core0': core0, 'core1': core1, 'end': weights_end}[move](*what)
+         'core0': core0, 'core1': core1, 'end': weights_end,
+         'out': weights_out}[move](*what)
 
     for w in range(4):
         part = tok_hbm.at[0, 0]
@@ -445,13 +453,14 @@
             @pl.when(c == core)
             def _():
                 for way in range(2):
-                    for step in (range(4 - way) if core == 0 else (2,)):
+                    for step in range(4 - way if core == 0 else 0):
                         wait_out(r, ring_send.at[way, step, a])
                 for label in labels(core):
                     wait_out(r, sib_send.at[label, a])
                 if core == 0:
-                    for label in range(len(lent)):
-                        wait_out(r, lend_send.at[label, a])
+                    wait_out(r, lend_send.at[6, a])
+        for step in range(3):
+            wait_out(r, lend_send.at[2 * step + odd, a])
     for w in range(4):
         for h in range(2):
             pltpu.make_async_copy(out_v.at[:, 4 * h + w], out_hbm.at[:, 4 * h + w], out_sem.at[w, h]).wait()
@@ -485,7 +494,7 @@
         pltpu.VMEM((256, 256), F32),
         dma((3,)), dma((4, 8)), dma((4, 8)), dma((4, 2)), dma((4, 2)), dma((4, 8)), dma((4, 2, 4)),
         dma((4, 4)), dma((4, 4)), dma((4, 4)), dma((4, 4)), dma((2, 2)), dma((2, 2)),
-        dma((2, 4, 2)), dma((2, 4, 2)), dma((13, 2)), dma((13, 2)), dma((5, 2)), dma((5, 2)), dma((4, 2)),
+        dma((2, 4, 2)), dma((2, 4, 2)), dma((15, 2)), dma((15, 2)), dma((7, 2)), dma((7, 2)), dma((4, 2)),
     ]
     any_space = pl.BlockSpec(memory_space=pl.ANY)
     vmem = pl.BlockSpec(memory_space=pltpu.VMEM)

time: 75.9 us -> 74.3 us (0.979)
  Pallas kernels: 73.3 us -> 71.5 us
    pallas_call x1, Pallas kernels: 73.3 us -> 71.5 us  [on_device(): pl.pallas_call(layer, out_shape=jax.ShapeDtypeStruct((4, 8, 16, D), BF),...]
where the time goes in v3:
time: 74.3 us; the launch traced here: 74 us
  Pallas kernels  71.5 us (96%)
  local copies, waits for them, and re-layouts  2.46 us (3%)
    pallas_call x1, Pallas kernels, on_device(): pl.pallas_call(layer, out_shape=jax.ShapeDtypeStruct((4, 8, 16, D), BF),...  71.5 us
    unnamed x1, local copies, waits for them, and re-layouts  2.46 us

profile of v3, /device:TPU:1, one launch (start us, length us, event | category | flops | bytes accessed | tf_op | source)
XLA Modules:
  0.0 74.0 jit_solution(17416583927307529045)
XLA Ops:
  0.0 71.5 %shard_map.82 = bf16[4,8,16,1280]{3,2,1,0:T(8,128)(2,1)} custom-call(bf16[4,8,16,1280]{3,2,1,0:T(8,128)(2,1)} %bitcast.4, bf16[1280,1920]{1,0:T(8,128)(2,1)} %swin_hbm.1, bf16[640,1280]{1,0:T(8,128)(2,1)} %swout_hbm.1, bf16[40,1920]{1,0:T(8,128)(2,1)} %tin_sh.1, bf16[20,1280]{1,0:T(8,128)(2,1)} %tout_sh.1, f32[1280]{0:T(1024)} %sgain.1, f32[1280]{0:T(1024)} %tgain.1, ...), custom_call_target="tpu_custom_call" | custom-call | tf_op jit(solution)/shard_map/pallas_call | solution.py:501
  71.5 2.5 %copy.10 = bf16[4,128,1280]{2,1,0:T(8,128)(2,1)} copy(bf16[4,128,1280]{2,1,0:T(8,128)(2,1)} %bitcast.3) | data formatting | bytes 2621440
